TPU v7x, 32 devices: a whole 2x2x4 slice. The times are simulated.
32 devices in a mesh: mesh: 4 (over y, core), mode: 8 (over z, x).
Axes of the slice: x: 2, y: 2, z: 4, core: 2. Of those that a mesh axis runs over, the one named last changes fastest.
Arguments:
- field: float32 [256, 512, 1024], P('mode', 'mesh'), may hold values from -6 to 6
- kappa: bfloat16 [3, 512, 1024], P(None, ('mesh', 'mode')), may hold values from 0.099609375 to 1
- mass: float32 [512, 1024], P(('mesh', 'mode')), may hold values from 0.5 to 1.5
- kl_modes: bfloat16 [3, 256, 256], replicated, may hold values from -0.375 to 0.375
- to_points: bfloat16 [512, 256], replicated, may hold values from -0.375 to 0.375
- from_points: bfloat16 [256, 512], replicated, may hold values from -0.25 to 0.25
- capacity: float32 [512], replicated, may hold values from 0.5 to 2
- latent: float32 [512], replicated, may hold values from 0.5 to 3
Outputs:
- residual: bfloat16 [256, 512, 1024], P('mode', 'mesh')
All inputs are finite; a program needn't handle non-finite values.
Results may differ from a plain program's by a relative error of at most 0.0058.
Values may be sent and summed in bfloat16 or wider, within the bound.
A program may use at most 256 MiB of HBM per device.

v0:
```python
import jax
import jax.numpy as jnp
from jax import lax
from jax.sharding import PartitionSpec as P


def extended(cells, sides, width):
    for axis, dim in sides:
        count = lax.axis_size(axis)
        ends = count - 1
        head = lax.slice_in_dim(cells, 0, width, axis=dim)
        tail = lax.slice_in_dim(cells, cells.shape[dim] - width, cells.shape[dim], axis=dim)
        cells = jnp.concatenate(
            [
                lax.ppermute(tail, axis, [(i, (i + 1) % count) for i in range(ends)]),
                cells,
                lax.ppermute(head, axis, [((i + 1) % count, i) for i in range(ends)]),
            ],
            axis=dim,
        )
    return cells


def conduct(values, kappa):
    count = values.shape[1] - 2
    width = values.shape[2]
    vals = jnp.pad(values.astype(jnp.float32), ((0, 0), (0, 0), (1, 1)))[None]
    kaps = jnp.pad(kappa.astype(jnp.float32), ((0, 0), (0, 0), (1, 1)))[:, None]
    centre = vals[:, :, 1 : 1 + count, 1 : 1 + width]
    kcentre = kaps[:, :, 1 : 1 + count, 1 : 1 + width]
    total = jnp.zeros((kaps.shape[0], vals.shape[1], count, width), jnp.float32)
    for shift_x, shift_y in ((0, 1), (2, 1), (1, 0), (1, 2)):
        other = vals[:, :, shift_x : shift_x + count, shift_y : shift_y + width]
        kother = kaps[:, :, shift_x : shift_x + count, shift_y : shift_y + width]
        total = total + 0.5 * (kcentre + kother) * (centre - other)
    return total.astype(jnp.bfloat16)


def finish(coarse, images, mass_rows, kl_modes, to_points, from_points, capacity, latent):
    mixed = jnp.einsum("kij,kjxy->ixy", kl_modes, images, preferred_element_type=jnp.float32)
    temps = jnp.einsum("qi,ixy->qxy", to_points, coarse, preferred_element_type=jnp.float32)
    heat = (
        capacity[:, None, None] * temps + latent[:, None, None] * jax.nn.sigmoid(2.0 * temps)
    ).astype(jnp.bfloat16)
    enthalpy = jnp.einsum("iq,qxy->ixy", from_points, heat, preferred_element_type=jnp.float32)
    return (mass_rows[None] * enthalpy + mixed).astype(jnp.bfloat16)


def body(field, kappa, mass, kl_modes, to_points, from_points, capacity, latent):
    coarse = field.astype(jnp.bfloat16)
    owned = coarse.shape[0]
    width = coarse.shape[2]
    groups = lax.axis_size("mode")
    terms = kappa.shape[0]
    kap_rows = lax.all_gather(kappa, "mode", axis=1, tiled=True)
    stacked = jnp.concatenate([coarse, kap_rows], 0)
    padded = extended(stacked, (("mesh", 1),), 1)
    images = conduct(padded[:owned], padded[owned:])
    joined = jnp.concatenate([coarse[None], images], 0)
    joined = joined.reshape((terms + 1) * owned, coarse.shape[1], width)
    moved = lax.all_to_all(joined, "mode", split_axis=1, concat_axis=0, tiled=True)
    node_rows = moved.shape[1]
    moved = moved.reshape(groups, terms + 1, owned, node_rows, width)
    moved = jnp.transpose(moved, (1, 0, 2, 3, 4)).reshape(
        terms + 1, groups * owned, node_rows, width
    )
    node_coarse = moved[0]
    node_images = moved[1:]
    result = finish(
        node_coarse, node_images, mass, kl_modes, to_points, from_points, capacity, latent
    )
    return lax.all_to_all(result, "mode", split_axis=0, concat_axis=1, tiled=True)


def solution(mesh):
    in_specs = (
        P("mode", "mesh", None),
        P(None, ("mesh", "mode"), None),
        P(("mesh", "mode"), None),
        P(),
        P(),
        P(),
        P(),
        P(),
    )
    out_specs = P("mode", "mesh", None)
    return jax.shard_map(body, mesh=mesh, in_specs=in_specs, out_specs=out_specs, check_vma=False)
```

profile of v0, /device:TPU:0, one launch (start us, length us, event | category | flops | bytes accessed | tf_op | source)
XLA Modules:
  0.0 1315.4 jit_solution(11272950333644281777)
XLA Ops:
  0.0 0.0 copy-start
  0.0 0.0 copy-start.2
  0.0 16.5 %copy.54 = bf16[32,128,1024]{2,0,1:T(8,128)(2,1)S(1)} copy(f32[32,128,1024]{2,1,0:T(8,128)} %param.8) | data formatting | bytes 25165824 | tf_op args[0]
  16.6 0.0 copy-done.2
  16.6 0.0 copy-start.1
  16.6 33.8 %all_gather.3 = bf16[3,128,1024]{2,1,0:T(8,128)(2,1)S(1)} all-gather(bf16[3,16,1024]{2,1,0:T(8,128)(2,1)S(1)} %copy-done.2), channel_id=1, replica_groups=mesh['mesh'=4,'mode'=8] {'mode'}, dimensions={1}, use_global_device_ids=true | all-gather | bytes 884736 | tf_op jit(solution)/shard_map/all_gather | solution.py:55
  50.4 0.7 copy.32
  51.1 0.0 slice-start.3
  51.1 1.6 collective-permute-start
  52.7 1.5 collective-permute-start.1
  54.2 0.0 slice-done
  54.2 0.0 slice-done.1
  54.2 0.0 slice-done.2
  54.3 0.0 slice-done.3
  54.3 11.4 copy.56
  65.7 0.0 collective-permute-done
  65.7 0.0 collective-permute-done.1
  65.7 0.0 copy-done.1
  65.7 12.0 fusion.11
  77.7 51.1 %fusion.6 = (f32[32,128,1024]{2,0,1:T(8,128)}, f32[32,128,1024]{2,0,1:T(8,128)}, f32[32,128,1024]{2,0,1:T(8,128)}, f32[32,128,1024]{2,0,1:T(8,128)}) fusion(f32[1,32,130,1026]{3,1,2,0:T(8,128)} %fusion.11), kind=kLoop, calls=%fused_computation.15 | loop fusion | flops 16777216 | bytes 150994944 | tf_op jit(solution)/shard_map/mul | solution.py:35
  128.8 2.9 fusion.38
  131.7 0.0 slice-start.6
  131.7 0.0 slice-start.7
  131.7 4.5 fusion.36
  136.2 0.0 slice-done.4
  136.2 0.0 slice-done.5
  136.2 0.0 slice-done.6
  136.2 0.0 slice-done.7
  136.3 46.6 %add_convert_fusion = bf16[3,32,128,1024]{3,1,0,2:T(8,128)(2,1)} fusion(f32[32,128,1024]{2,0,1:T(8,128)} %get-tuple-element.8, f32[3,128,1024]{2,0,1:T(4,128)S(1)} %get-tuple-element.14, f32[32,128,1024]{2,0,1:T(8,128)} %get-tuple-element.6, f32[3,128,1024]{2,0,1:T(4,128)S(1)} %get-tuple-element.12, f32[32,128,1024]{2,0,1:T(8,128)} %get-tuple-element.7, ...), kind=kLoop, calls=%fused_computation | loop fusion | flops 100663296 | bytes 98566144 | tf_op jit(solution)/shard_map/convert_element_type | solution.py:36
  182.9 23.1 %pad_maximum_fusion = bf16[4,32,128,1024]{3,1,0,2:T(8,128)(2,1)} fusion(bf16[3,32,128,1024]{3,1,0,2:T(8,128)(2,1)} %add_convert_fusion, bf16[1,32,128,1024]{3,1,0,2:T(8,128)(2,1)} %bitcast.79), kind=kLoop, calls=%fused_computation.1 | loop fusion | flops 16777216 | bytes 67108864 | tf_op jit(solution)/shard_map/concatenate | solution.py:59
  205.9 734.0 %all_to_all.33 = bf16[128,128,1024]{2,0,1:T(8,128)(2,1)} all-to-all(bf16[128,128,1024]{2,0,1:T(8,128)(2,1)} %bitcast.72), channel_id=1, replica_groups=mesh['mesh'=4,'mode'=8] {'mode'}, dimensions={1} | all-to-all | bytes 67108864 | tf_op jit(solution)/shard_map/all_to_all | solution.py:61
  939.9 30.8 %copy.35 = bf16[8,128,16,1024]{3,2,1,0:T(8,128)(2,1)} copy(bf16[8,128,16,1024]{3,1,2,0:T(8,128)(2,1)} %bitcast.73) | data formatting | bytes 67108864 | tf_op jit(solution)/shard_map/all_to_all | solution.py:61
  970.8 21.4 %slice.80 = bf16[3,8,32,16,1024]{4,3,2,0,1:T(8,128)(2,1)} slice(bf16[4,8,32,16,1024]{4,3,2,0,1:T(8,128)(2,1)} %bitcast.70), slice={[1:4], [0:8], [0:32], [0:16], [0:1024]} | slice | bytes 50331648 | tf_op jit(solution)/shard_map/slice | solution.py:68
  992.2 8.7 slice.79
  1000.9 21.3 %copy.37 = bf16[3,8,32,16,1024]{4,3,2,1,0:T(8,128)(2,1)} copy(bf16[3,8,32,16,1024]{4,3,2,0,1:T(8,128)(2,1)} %slice.80) | data formatting | bytes 50331648 | tf_op jit(solution)/shard_map/slice | solution.py:68
  1022.2 0.0 copy-done
  1022.2 0.0 copy-start.5
  1022.2 0.0 copy-start.6
  1022.2 0.0 copy-start.7
  1022.2 59.9 %fusion = f32[16,1024,256,1]{2,1,3,0:T(8,128)} fusion(bf16[3,256,16,1024]{3,2,1,0:T(8,128)(2,1)} %bitcast.80, bf16[3,256,256]{2,1,0:T(8,128)(2,1)S(1)} %copy-done), kind=kOutput, calls=%fused_computation.5 | convolution fusion | flops 6442450944 | bytes 42336256 | tf_op jit(solution)/shard_map/kij,kjxy->ixy/dot_general | solution.py:40
  1082.1 0.0 copy-done.3
  1082.2 0.0 copy-done.4
  1082.2 0.0 copy-done.5
  1082.2 0.0 copy-done.6
  1082.2 22.9 %fusion.23 = bf16[256,16,1024]{0,2,1:T(8,128)(2,1)} fusion(f32[16,1024,256,1]{2,1,3,0:T(8,128)} %fusion, f32[512]{0:T(512)S(1)} %copy-done.6, f32[512]{0:T(512)S(1)} %copy-done.7, bf16[256,16,1024]{2,1,0:T(8,128)(2,1)} %bitcast.81, f32[16,1024]{1,0:T(8,128)S(1)} %copy-done.5, bf16[256,512]{1,0:T(8,128)(2,1)S(1)} %copy-done.3, bf16[512,256]{1,0:T(8,128)(2,1)S(1)} %copy-done.4), kind=kOutput, calls=%fused_computation.30 | convolution fusion | flops 8669626368 | bytes 34148352 | tf_op jit(solution)/shard_map/iq,qxy->ixy/dot_general | solution.py:45
  1105.1 12.2 copy.39
  1117.3 189.1 %all_to_all.34 = bf16[256,16,1024]{2,1,0:T(8,128)(2,1)} all-to-all(bf16[256,16,1024]{2,1,0:T(8,128)(2,1)} %copy.39), channel_id=1, replica_groups=mesh['mesh'=4,'mode'=8] {'mode'}, dimensions={0} | all-to-all | bytes 16777216 | tf_op jit(solution)/shard_map/all_to_all | solution.py:72
  1306.4 8.7 copy.40
  (11 shorter events, 0.0 us)
Async XLA Ops:
  0.0 1022.2 %copy-start = (bf16[3,256,256]{2,1,0:T(8,128)(2,1)S(1)}, bf16[3,256,256]{2,1,0:T(8,128)(2,1)}, u32[]{:S(2)}) copy-start(bf16[3,256,256]{2,1,0:T(8,128)(2,1)} %param.11) | copy-start | bytes 1179652
  0.0 54.2 %slice-start = ((s8[16777216]{0:T(1024)(128)(4,1)}), s8[4194304]{0:T(1024)(128)(4,1)S(1)}, s32[]{:S(2)}) async-start(s8[16777216]{0:T(1024)(128)(4,1)} %bitcast.74), calls=%async_computation.2 | async-start | bytes 8388608
  0.0 54.2 %slice-start.1 = ((s8[16777216]{0:T(1024)(128)(4,1)}), s8[4194304]{0:T(1024)(128)(4,1)S(1)}, s32[]{:S(2)}) async-start(s8[16777216]{0:T(1024)(128)(4,1)} %bitcast.74), calls=%async_computation.3 | async-start | bytes 8388608
  0.0 54.2 %slice-start.2 = ((s8[16777216]{0:T(1024)(128)(4,1)}), s8[4194304]{0:T(1024)(128)(4,1)S(1)}, s32[]{:S(2)}) async-start(s8[16777216]{0:T(1024)(128)(4,1)} %bitcast.74), calls=%async_computation.4 | async-start | bytes 8388608
  0.0 16.6 %copy-start.2 = (bf16[3,16,1024]{2,1,0:T(8,128)(2,1)S(1)}, bf16[3,16,1024]{2,1,0:T(8,128)(2,1)}, u32[]{:S(2)}) copy-start(bf16[3,16,1024]{2,1,0:T(8,128)(2,1)} %param.9) | copy-start | bytes 294916
  16.6 49.1 %copy-start.1 = (bf16[32,128,1024]{2,0,1:T(8,128)(2,1)}, bf16[32,128,1024]{2,0,1:T(8,128)(2,1)S(1)}, u32[]{:S(2)}) copy-start(bf16[32,128,1024]{2,0,1:T(8,128)(2,1)S(1)} %copy.54) | copy-start | bytes 25165828
  51.1 3.2 slice-start.3
  51.1 14.6 %collective-permute-start = (bf16[35,1,1024]{2,0,1:T(8,128)(2,1)S(1)}, bf16[35,1,1024]{2,0,1:T(8,128)(2,1)S(1)}, u32[]{:S(2)}, u32[]{:S(2)}) collective-permute-start(bf16[35,1,1024]{2,0,1:T(8,128)(2,1)S(1)} %get-tuple-element.9), channel_id=1, source_target_pairs={{0,8},{8,16},{16,24},{1,9},{9,17},{17,25},{2,10},{10,18},{18,26},{... | collective-permute-start | bytes 215048 | tf_op jit(solution)/shard_map/ppermute | solution.py:15
  52.7 13.0 collective-permute-start.1
  128.8 7.5 slice-start.4
  128.8 7.5 slice-start.5
  131.7 4.6 slice-start.6
  131.7 4.6 slice-start.7
  1022.2 60.0 %copy-start.3 = (bf16[256,512]{1,0:T(8,128)(2,1)S(1)}, bf16[256,512]{1,0:T(8,128)(2,1)}, u32[]{:S(2)}) copy-start(bf16[256,512]{1,0:T(8,128)(2,1)} %param.13) | copy-start | bytes 786436
  1022.2 60.0 %copy-start.4 = (bf16[512,256]{1,0:T(8,128)(2,1)S(1)}, bf16[512,256]{1,0:T(8,128)(2,1)}, u32[]{:S(2)}) copy-start(bf16[512,256]{1,0:T(8,128)(2,1)} %param.12) | copy-start | bytes 786436
  1022.2 60.0 %copy-start.5 = (f32[16,1024]{1,0:T(8,128)S(1)}, f32[16,1024]{1,0:T(8,128)}, u32[]{:S(2)}) copy-start(f32[16,1024]{1,0:T(8,128)} %param.10) | copy-start | bytes 196612
  1022.2 60.0 %copy-start.6 = (f32[512]{0:T(512)S(1)}, f32[512]{0:T(512)}, u32[]{:S(2)}) copy-start(f32[512]{0:T(512)} %param.15) | copy-start | bytes 6148
  1022.2 60.0 %copy-start.7 = (f32[512]{0:T(512)S(1)}, f32[512]{0:T(512)}, u32[]{:S(2)}) copy-start(f32[512]{0:T(512)} %param.14) | copy-start | bytes 6148
where the time goes:
time: 1320 us
  blocking collectives  957 us (72%)
  other arithmetic  140 us (11%)
  local copies, waits for them, and re-layouts  132 us (10%)
  matrix products  82.8 us (6%)
    all_to_all x1, blocking collectives, body(): lax.all_to_all(joined, 'mode', split_axis=1, concat_axis=0, tiled=True)  734 us
    all_to_all x1, blocking collectives, body(): lax.all_to_all(result, 'mode', split_axis=0, concat_axis=1, tiled=True)  189 us
    dot_general x1, matrix products, finish(): jnp.einsum('kij,kjxy->ixy', kl_modes, images, preferred_element_type=jnp....  59.9 us
    mul x2, other arithmetic, conduct(): total = total + 0.5 * (kcentre + kother) * (centre - other)  55.6 us
    convert_element_type x1, other arithmetic, conduct(): return total.astype(jnp.bfloat16)  46.6 us
    slice x2, local copies, waits for them, and re-layouts, body(): node_images = moved[1:]  42.7 us
    all_gather x1, blocking collectives, body(): kap_rows = lax.all_gather(kappa, 'mode', axis=1, tiled=True)  33.8 us
    all_to_all x1, local copies, waits for them, and re-layouts, body(): lax.all_to_all(joined, 'mode', split_axis=1, concat_axis=0, tiled=True)  30.8 us
  transfers between devices with their start and end apart: 2, of which 0 were waited for; matrix products, arithmetic and copies ran while one was open for 1% of the time, Pallas kernels for 0%

commit v1 on v0

v1 whole, which is shorter than its diff:
```python
import functools

import jax
import jax.numpy as jnp
from jax import lax
from jax.experimental import pallas as pl
from jax.experimental.pallas import tpu as pltpu
from jax.sharding import PartitionSpec as P

STEP = 2
BAND = 16
TILE = 256


def halo(rows, axes):
    count = lax.axis_size(axes)
    up = lax.ppermute(rows[-1:], axes, [(i, i + 1) for i in range(count - 1)])
    down = lax.ppermute(rows[:1], axes, [(i + 1, i) for i in range(count - 1)])
    return up, down


def weights_of(kappa):
    rows = jnp.moveaxis(kappa, 1, 0)
    up, down = halo(rows, ("mesh", "mode"))
    ext = jnp.concatenate([up, rows, down], 0).astype(jnp.float32)
    count, terms, width = rows.shape
    ext = jnp.pad(ext, ((0, 0), (0, 0), (1, 1)))
    centre = ext[1:-1, :, 1:-1]
    others = (ext[:-2, :, 1:-1], ext[2:, :, 1:-1], ext[1:-1, :, :-2], ext[1:-1, :, 2:])
    return jnp.stack([0.5 * (centre + other) for other in others], 2).reshape(count, terms * 4, width)


def kernel(groups, src, coef, mass, kl, tp, fp, cap, lat, out, gath, res, img, recv_in, send_in, send_out, recv_out):
    me = lax.axis_index("mode")
    owned = src.shape[1]
    width = src.shape[2]
    nrows = res.shape[0]
    modes = res.shape[1]
    terms = coef.shape[1] // 4
    steps = nrows // STEP
    peers = [lax.rem(me + s, groups) for s in range(1, groups)]
    mine = pl.ds(pl.multiple_of(me * owned, owned), owned)
    others = pl.ds(0, modes - owned)

    barrier = pltpu.get_barrier_semaphore()
    for peer in peers:
        pl.semaphore_signal(barrier, inc=1, device_id={"mode": peer}, device_id_type=pl.DeviceIdType.MESH)
    pl.semaphore_wait(barrier, groups - 1)

    def send_chunk(c, carry):
        here = pl.ds(c * STEP, STEP)
        for peer in peers:
            pltpu.make_async_remote_copy(
                src_ref=src.at[pl.ds(peer * nrows + c * STEP, STEP)],
                dst_ref=gath.at[here, mine, :],
                send_sem=send_in,
                recv_sem=recv_in.at[c],
                device_id={"mode": peer},
                device_id_type=pl.DeviceIdType.MESH,
            ).start()
        pltpu.make_async_copy(
            src.at[pl.ds(me * nrows + c * STEP, STEP)], gath.at[here, mine, :], recv_in.at[c]
        ).start()
        return carry

    lax.fori_loop(0, steps + 1, send_chunk, 0)

    def wait_chunk(c):
        part = gath.at[pl.ds(c * STEP, STEP)]
        pltpu.make_async_copy(part, part, recv_in.at[c]).wait()

    wait_chunk(0)
    cols = lax.broadcasted_iota(jnp.int32, (BAND, width), 1)
    first = cols == 0
    last = cols == width - 1

    def row(r):
        @pl.loop(0, modes // BAND)
        def _(b):
            band = pl.ds(pl.multiple_of(b * BAND, BAND), BAND)
            v = gath[r + 1, band, :].astype(jnp.float32)
            diffs = (
                v - gath[r, band, :].astype(jnp.float32),
                v - gath[r + 2, band, :].astype(jnp.float32),
                v - jnp.where(first, 0.0, pltpu.roll(v, 1, 1)),
                v - jnp.where(last, 0.0, pltpu.roll(v, width - 1, 1)),
            )
            for k in range(terms):
                total = coef[r, 4 * k : 4 * k + 1, :] * diffs[0]
                for d in range(1, 4):
                    total = total + coef[r, 4 * k + d : 4 * k + d + 1, :] * diffs[d]
                img[pl.ds(pl.multiple_of(k * modes + b * BAND, BAND), BAND), :] = total.astype(jnp.bfloat16)

        @pl.loop(0, width // TILE)
        def _(t):
            tile = pl.ds(pl.multiple_of(t * TILE, TILE), TILE)
            temps = jnp.dot(tp[...], gath[r + 1, :, tile], preferred_element_type=jnp.float32)
            half = lat[...] * 0.5
            heat = (cap[...] * temps + (half + half * jnp.tanh(temps))).astype(jnp.bfloat16)
            enthalpy = jnp.dot(fp[...], heat, preferred_element_type=jnp.float32)
            mixed = jnp.dot(kl[...], img[:, tile], preferred_element_type=jnp.float32)
            res[r, :, tile] = (mass[r, :, tile] * enthalpy + mixed).astype(jnp.bfloat16)

    def step(p, carry):
        wait_chunk(p + 1)

        @pl.loop(0, STEP)
        def _(i):
            row(p * STEP + i)

        here = pl.ds(p * STEP, STEP)
        there = out.at[pl.ds(me * nrows + p * STEP, STEP)]
        for peer in peers:
            pltpu.make_async_remote_copy(
                src_ref=res.at[here, pl.ds(pl.multiple_of(peer * owned, owned), owned), :],
                dst_ref=there,
                send_sem=send_out,
                recv_sem=recv_out,
                device_id={"mode": peer},
                device_id_type=pl.DeviceIdType.MESH,
            ).start()
        pltpu.make_async_copy(res.at[here, mine, :], there, recv_out).start()
        return carry

    lax.fori_loop(0, steps, step, 0)

    sent = gath.at[:, others, :]
    pltpu.make_async_copy(sent, sent, send_in).wait()
    sent = res.at[:, others, :]
    pltpu.make_async_copy(sent, sent, send_out).wait()
    pltpu.make_async_copy(out, out, recv_out).wait()


def exchange(ext, coef, mass, kl, tp, fp, cap, lat):
    groups = lax.axis_size("mode")
    owned, width = ext.shape[1:]
    nrows, modes = mass.shape[0], tp.shape[1]
    vmem = pl.BlockSpec(memory_space=pltpu.VMEM)
    hbm = pl.BlockSpec(memory_space=pl.ANY)
    work = modes * nrows * width
    return pl.pallas_call(
        functools.partial(kernel, groups),
        out_shape=jax.ShapeDtypeStruct((nrows * groups, owned, width), jnp.bfloat16),
        in_specs=[hbm] + [vmem] * 7,
        out_specs=hbm,
        scratch_shapes=[
            pltpu.VMEM((nrows + STEP, modes, width), jnp.bfloat16),
            pltpu.VMEM((nrows, modes, width), jnp.bfloat16),
            pltpu.VMEM((kl.shape[1], width), jnp.bfloat16),
            pltpu.SemaphoreType.DMA((nrows // STEP + 1,)),
            pltpu.SemaphoreType.DMA,
            pltpu.SemaphoreType.DMA,
            pltpu.SemaphoreType.DMA,
        ],
        compiler_params=pltpu.CompilerParams(
            collective_id=0, has_side_effects=True, vmem_limit_bytes=44 * 1024 * 1024
        ),
        cost_estimate=pl.CostEstimate(
            flops=2 * work * (kl.shape[1] + 2 * tp.shape[0]),
            bytes_accessed=4 * work,
            transcendentals=nrows * width * tp.shape[0],
        ),
    )(ext, coef, mass[:, None, :], kl, tp, fp, cap[:, None], lat[:, None])


def exchange_small(ext, coef, mass, kl, tp, fp, cap, lat):
    groups = lax.axis_size("mode")
    owned, width = ext.shape[1:]
    nrows, modes = mass.shape[0], tp.shape[1]
    terms = coef.shape[1] // 4
    parts = jnp.stack([ext[d * nrows : d * nrows + nrows + 2] for d in range(groups)], 0)
    moved = lax.all_to_all(parts, "mode", split_axis=0, concat_axis=0, tiled=True)
    rows = jnp.moveaxis(moved, 0, 1).reshape(nrows + 2, modes, width)
    own = rows[1:-1]
    v = jnp.pad(rows.astype(jnp.float32), ((0, 0), (0, 0), (1, 1)))
    centre = v[1:-1, :, 1:-1]
    others = (v[:-2, :, 1:-1], v[2:, :, 1:-1], v[1:-1, :, :-2], v[1:-1, :, 2:])
    images = [
        sum(coef[:, 4 * k + d, None, :] * (centre - others[d]) for d in range(4)).astype(jnp.bfloat16)
        for k in range(terms)
    ]
    images = jnp.concatenate(images, 1)
    mixed = jnp.einsum("ij,rjx->rix", kl, images, preferred_element_type=jnp.float32)
    temps = jnp.einsum("qi,rix->rqx", tp, own, preferred_element_type=jnp.float32)
    heat = (cap[:, None] * temps + lat[:, None] * jax.nn.sigmoid(2.0 * temps)).astype(jnp.bfloat16)
    enthalpy = jnp.einsum("iq,rqx->rix", fp, heat, preferred_element_type=jnp.float32)
    result = (mass[:, None, :] * enthalpy + mixed).astype(jnp.bfloat16)
    result = result.reshape(nrows, groups, owned, width)
    back = lax.all_to_all(result, "mode", split_axis=1, concat_axis=0, tiled=True)
    return back.reshape(nrows * groups, owned, width)


def body(field, kappa, mass, kl_modes, to_points, from_points, capacity, latent):
    coarse = jnp.transpose(field.astype(jnp.bfloat16), (1, 0, 2))
    up, down = halo(coarse, "mesh")
    ext = jnp.concatenate([up, coarse, down], 0)
    coef = weights_of(kappa)
    terms, modes = kl_modes.shape[:2]
    kl = jnp.transpose(kl_modes, (1, 0, 2)).reshape(modes, terms * modes)
    nrows, owned = mass.shape[0], field.shape[0]
    fits = owned % 16 == 0 and nrows % STEP == 0 and field.shape[2] % TILE == 0
    run = exchange if fits else exchange_small
    out = run(ext, coef, mass, kl, to_points, from_points, capacity, latent)
    return jnp.transpose(out, (1, 0, 2))


def solution(mesh):
    in_specs = (
        P("mode", "mesh", None),
        P(None, ("mesh", "mode"), None),
        P(("mesh", "mode"), None),
        P(),
        P(),
        P(),
        P(),
        P(),
    )
    out_specs = P("mode", "mesh", None)
    return jax.shard_map(body, mesh=mesh, in_specs=in_specs, out_specs=out_specs, check_vma=False)
```

time: 1320 us -> 443 us (0.34)
  blocking collectives: 957 us -> 0 us
  Pallas kernels: 0 us -> 379 us
  other arithmetic: 140 us -> 7.73 us
  local copies, waits for them, and re-layouts: 132 us -> 33.3 us
  matrix products: 82.8 us -> 0 us
    all_to_all x2 -> x0, blocking collectives: 923 us -> none  [the longest x1 734 us: body(): lax.all_to_all(joined, 'mode', split_axis=1, concat_axis=0, tiled=True)]
    pallas_call x0 -> x1, Pallas kernels: none -> 379 us  [exchange(): pl.pallas_call(functools.partial(kernel, groups), out_shape=jax.ShapeDtyp...]
    dot_general x2 -> x0, matrix products: 82.8 us -> none  [the longest x1 59.9 us: finish(): jnp.einsum('kij,kjxy->ixy', kl_modes, images, preferred_element_type=jnp....]
    mul x2 -> x0, other arithmetic: 55.6 us -> none  [conduct(): total = total + 0.5 * (kcentre + kother) * (centre - other)]
    slice x3 -> x2, local copies, waits for them, and re-layouts: 51.4 us -> 0.85 us  [halo(): up = lax.ppermute(rows[-1:], axes, [(i, i + 1) for i in range(count - 1)])]
    convert_element_type x1, other arithmetic: 46.6 us -> 0.06 us  [weights_of(): ext = jnp.concatenate([up, rows, down], 0).astype(jnp.float32)]
    all_to_all x2 -> x0, local copies, waits for them, and re-layouts: 39.5 us -> none  [the longest x1 30.8 us: body(): lax.all_to_all(joined, 'mode', split_axis=1, concat_axis=0, tiled=True)]
    all_gather x1 -> x0, blocking collectives: 33.8 us -> none  [body(): kap_rows = lax.all_gather(kappa, 'mode', axis=1, tiled=True)]
  transfers between devices with their start and end apart: 2 -> 4, of which waited for: 0 -> 1; matrix products, arithmetic and copies ran while one was open for 1% -> 4% of each run, Pallas kernels for 0% -> 0%
where the time goes in v1:
time: 443 us; the launch traced here: 436 us
  Pallas kernels  379 us (86%)
  local copies, waits for them, and re-layouts  33.3 us (8%)
  starting transfers between devices  13.3 us (3%)
  other arithmetic  7.73 us (2%)
    pallas_call x1, Pallas kernels, exchange(): pl.pallas_call(functools.partial(kernel, groups), out_shape=jax.ShapeDtyp...  379 us
    unnamed x18, local copies, waits for them, and re-layouts  20 us
    transpose x1, local copies, waits for them, and re-layouts, body(): return jnp.transpose(out, (1, 0, 2))  11.5 us
    ppermute x2, starting transfers between devices, halo(): up = lax.ppermute(rows[-1:], axes, [(i, i + 1) for i in range(count - 1)])  10.5 us
  transfers between devices with their start and end apart: 4, of which 1 were waited for; matrix products, arithmetic and copies ran while one was open for 4% of the time, Pallas kernels for 0%

profile of v1, /device:TPU:0, one launch (start us, length us, event | category | flops | bytes accessed | tf_op | source)
XLA Modules:
  0.0 435.6 jit_solution(16409932110236762606)
XLA Ops:
  0.0 0.8 fusion.12
  0.8 4.8 %collective-permute-start.2 = (bf16[1,3,1024]{2,0,1:T(2,128)(2,1)S(1)}, bf16[1,3,1024]{2,0,1:T(2,128)(2,1)S(1)}, u32[]{:S(2)}, u32[]{:S(2)}) collective-permute-start(bf16[1,3,1024]{2,0,1:T(2,128)(2,1)S(1)} %get-tuple-element.11), channel_id=1, source_target_pairs={{0,1},{1,2},{2,3},{3,4},{4,5},{5,6},{6,7},{7,8},{8,9},{9,10},{10,1... | collective-permute-start | bytes 18440 | tf_op jit(solution)/shard_map/ppermute | solution.py:17
  5.7 0.0 copy-start.3
  5.7 0.0 copy-start.6
  5.7 0.0 copy-start.7
  5.7 0.0 copy-start.5
  5.7 0.0 copy-start.4
  5.8 1.4 collective-permute-start.3
  7.2 16.4 %copy.26 = bf16[32,128,1024]{2,0,1:T(8,128)(2,1)S(1)} copy(f32[32,128,1024]{2,1,0:T(8,128)} %param.8) | data formatting | bytes 25165824 | tf_op args[0]
  23.6 0.0 copy-start.2
  23.6 3.4 copy-done.2
  27.0 5.7 %collective-permute-start = (bf16[1,32,1024]{2,1,0:T(8,128)(2,1)S(1)}, bf16[1,32,1024]{2,1,0:T(8,128)(2,1)S(1)}, u32[]{:S(2)}, u32[]{:S(2)}) collective-permute-start(bf16[1,32,1024]{2,1,0:T(8,128)(2,1)S(1)} %get-tuple-element.5), channel_id=1, source_target_pairs={{0,8},{8,16},{16,24},{1,9},{9,17},{17,25},{2,10},{10,18},{18,26},{... | collective-permute-start | bytes 196616 | tf_op jit(solution)/shard_map/ppermute | solution.py:17
  32.7 1.3 collective-permute-start.1
  34.0 0.0 copy-done.3
  34.0 0.2 copy.17
  34.2 0.2 copy.19.kl
  34.3 0.0 copy-done.6
  34.3 0.1 copy.20.cap
  34.5 0.0 copy-done.7
  34.5 0.1 copy.21.lat
  34.7 0.0 copy-done.5
  34.7 0.0 collective-permute-done.2
  34.7 0.0 collective-permute-done.3
  34.7 0.0 copy-done.4
  34.8 0.1 maximum_convert_fusion
  34.8 0.2 fusion.10
  35.0 0.1 pad_maximum_fusion.1
  35.1 0.5 copy.18.coef
  35.6 0.0 copy-start
  35.6 0.0 copy-start.1
  35.6 0.0 collective-permute-done
  35.6 2.1 collective-permute-done.1
  37.6 7.4 %pad_maximum_fusion.src = bf16[130,32,1024]{2,1,0:T(8,128)(2,1)} fusion(bf16[1,32,1024]{2,1,0:T(8,128)(2,1)S(1)} %collective-permute-done.1, bf16[128,32,1024]{2,1,0:T(8,128)(2,1)} %bitcast.26, bf16[1,32,1024]{2,1,0:T(8,128)(2,1)S(1)} %collective-permute-done), kind=kLoop, calls=%fused_computation.1 | loop fusion | flops 8519680 | bytes 17039360 | tf_op jit(solution)/shard_map/concatenate | solution.py:196
  45.1 0.0 copy-done
  45.1 0.0 copy-done.1
  45.1 379.0 %shard_map.82 = bf16[128,32,1024]{2,1,0:T(8,128)(2,1)} custom-call(bf16[130,32,1024]{2,1,0:T(8,128)(2,1)} %pad_maximum_fusion.src, f32[16,12,1024]{2,1,0:T(8,128)S(1)} %copy.18.coef, f32[16,1,1024]{2,1,0:T(1,128)S(1)} %broadcast_in_dim.9.mass, bf16[256,768]{1,0:T(8,128)(2,1)S(1)} %copy.19.kl, bf16[512,256]{1,0:T(8,128)(2,1)S(1)} %copy-done, ...), custom_call_target="tpu_custom_call" | custom-call | flops 15032385536 | bytes 16777216 | tf_op jit(solution)/shard_map/pallas_call | solution.py:141
  424.1 11.5 %copy.22 = bf16[32,128,1024]{2,1,0:T(8,128)(2,1)} copy(bf16[32,128,1024]{2,0,1:T(8,128)(2,1)} %bitcast.27) | data formatting | bytes 16777216 | tf_op jit(solution)/shard_map/transpose | solution.py:204
  (2 shorter events, 0.1 us)
Async XLA Ops:
  0.8 33.9 %collective-permute-start.2 = (bf16[1,3,1024]{2,0,1:T(2,128)(2,1)S(1)}, bf16[1,3,1024]{2,0,1:T(2,128)(2,1)S(1)}, u32[]{:S(2)}, u32[]{:S(2)}) collective-permute-start(bf16[1,3,1024]{2,0,1:T(2,128)(2,1)S(1)} %get-tuple-element.11), channel_id=1, source_target_pairs={{0,1},{1,2},{2,3},{3,4},{4,5},{5,6},{6,7},{7,8},{8,9},{9,10},{10,1... | collective-permute-start | bytes 18440 | tf_op jit(solution)/shard_map/ppermute | solution.py:17
  5.7 28.3 %copy-start.3 = (bf16[3,256,256]{2,1,0:T(8,128)(2,1)S(1)}, bf16[3,256,256]{2,1,0:T(8,128)(2,1)}, u32[]{:S(2)}) copy-start(bf16[3,256,256]{2,1,0:T(8,128)(2,1)} %param.11) | copy-start | bytes 1179652
  5.7 28.6 %copy-start.6 = (f32[512]{0:T(512)S(1)}, f32[512]{0:T(512)}, u32[]{:S(2)}) copy-start(f32[512]{0:T(512)} %param.14) | copy-start | bytes 6148
  5.7 28.8 %copy-start.7 = (f32[512]{0:T(512)S(1)}, f32[512]{0:T(512)}, u32[]{:S(2)}) copy-start(f32[512]{0:T(512)} %param.15) | copy-start | bytes 6148
  5.7 28.9 %copy-start.5 = (f32[16,1024]{1,0:T(8,128)S(1)}, f32[16,1024]{1,0:T(8,128)}, u32[]{:S(2)}) copy-start(f32[16,1024]{1,0:T(8,128)} %param.10) | copy-start | bytes 196612
  5.7 29.0 %copy-start.4 = (bf16[3,16,1024]{2,1,0:T(8,128)(2,1)S(1)}, bf16[3,16,1024]{2,1,0:T(8,128)(2,1)}, u32[]{:S(2)}) copy-start(bf16[3,16,1024]{2,1,0:T(8,128)(2,1)} %param.9) | copy-start | bytes 294916
  5.8 29.0 %collective-permute-start.3 = (bf16[1,3,1024]{2,0,1:T(2,128)(2,1)S(1)}, bf16[1,3,1024]{2,0,1:T(2,128)(2,1)S(1)}, u32[]{:S(2)}, u32[]{:S(2)}) collective-permute-start(bf16[1,3,1024]{2,0,1:T(2,128)(2,1)S(1)} %get-tuple-element.12), channel_id=1, source_target_pairs={{1,0},{2,1},{3,2},{4,3},{5,4},{6,5},{7,6},{8,7},{9,8},{10,9},{11,1... | collective-permute-start | bytes 18440 | tf_op jit(solution)/shard_map/ppermute | solution.py:18
  23.6 3.4 copy-start.2
  27.0 8.6 %collective-permute-start = (bf16[1,32,1024]{2,1,0:T(8,128)(2,1)S(1)}, bf16[1,32,1024]{2,1,0:T(8,128)(2,1)S(1)}, u32[]{:S(2)}, u32[]{:S(2)}) collective-permute-start(bf16[1,32,1024]{2,1,0:T(8,128)(2,1)S(1)} %get-tuple-element.5), channel_id=1, source_target_pairs={{0,8},{8,16},{16,24},{1,9},{9,17},{17,25},{2,10},{10,18},{18,26},{... | collective-permute-start | bytes 196616 | tf_op jit(solution)/shard_map/ppermute | solution.py:17
  32.7 5.0 %collective-permute-start.1 = (bf16[1,32,1024]{2,1,0:T(8,128)(2,1)S(1)}, bf16[1,32,1024]{2,1,0:T(8,128)(2,1)S(1)}, u32[]{:S(2)}, u32[]{:S(2)}) collective-permute-start(bf16[1,32,1024]{2,1,0:T(8,128)(2,1)S(1)} %get-tuple-element.6), channel_id=1, source_target_pairs={{8,0},{16,8},{24,16},{9,1},{17,9},{25,17},{10,2},{18,10},{26,18},{... | collective-permute-start | bytes 196616 | tf_op jit(solution)/shard_map/ppermute | solution.py:18
  35.6 9.5 %copy-start = (bf16[512,256]{1,0:T(8,128)(2,1)S(1)}, bf16[512,256]{1,0:T(8,128)(2,1)}, u32[]{:S(2)}) copy-start(bf16[512,256]{1,0:T(8,128)(2,1)} %tp.1) | copy-start | bytes 786436
  35.6 9.5 %copy-start.1 = (bf16[256,512]{1,0:T(8,128)(2,1)S(1)}, bf16[256,512]{1,0:T(8,128)(2,1)}, u32[]{:S(2)}) copy-start(bf16[256,512]{1,0:T(8,128)(2,1)} %fp.1) | copy-start | bytes 786436

commit v2 on v1

v2 whole, which is shorter than its diff:
```python
import functools

import jax
import jax.numpy as jnp
from jax import lax
from jax.experimental import pallas as pl
from jax.experimental.pallas import tpu as pltpu
from jax.sharding import PartitionSpec as P

LOAD = 8
BAND = 16
TILE = 256


def halo(rows, axes):
    count = lax.axis_size(axes)
    up = lax.ppermute(rows[-1:], axes, [(i, i + 1) for i in range(count - 1)])
    down = lax.ppermute(rows[:1], axes, [(i + 1, i) for i in range(count - 1)])
    return up, down


def weights_of(kappa):
    rows = jnp.moveaxis(kappa, 1, 0)
    up, down = halo(rows, ("mesh", "mode"))
    ext = jnp.concatenate([up, rows, down], 0).astype(jnp.float32)
    count, terms, width = rows.shape
    ext = jnp.pad(ext, ((0, 0), (0, 0), (1, 1)))
    centre = ext[1:-1, :, 1:-1]
    others = (ext[:-2, :, 1:-1], ext[2:, :, 1:-1], ext[1:-1, :, :-2], ext[1:-1, :, 2:])
    return jnp.stack([0.5 * (centre + other) for other in others], 2).reshape(count, terms * 4, width)


def kernel(
    groups, parts, field, kap, mass, kl, tp, fp, cap, lat, out,
    buf, stage, gath, res, img, coef, kext,
    load, recv_rows, recv_halo, recv_kap, recv_out, send_in, send_edge, send_fwd, send_kap, send_out,
):
    me = lax.axis_index("mode")
    part = lax.axis_index("mesh")
    owned = field.shape[0]
    width = field.shape[2]
    nrows, modes = res.shape[:2]
    total_rows = nrows * groups
    terms = kap.shape[0]
    blocks = nrows // LOAD
    middle = groups // 2
    mine = pl.ds(pl.multiple_of(me * owned, owned), owned)
    others = pl.ds(0, modes - owned)
    peers = [lax.rem(me + s, groups) for s in range(1, groups)]
    has_prev = part > 0
    has_next = part < parts - 1
    opens = jnp.logical_or(me > 0, has_prev)
    closes = jnp.logical_or(me < groups - 1, has_next)

    def remote(src, dst, send, recv, device):
        return pltpu.make_async_remote_copy(
            src_ref=src, dst_ref=dst, send_sem=send, recv_sem=recv,
            device_id=device, device_id_type=pl.DeviceIdType.MESH,
        )

    def arrived(ref, sem):
        pltpu.make_async_copy(ref, ref, sem).wait()

    def block_load(i):
        peer = lax.rem(me + middle + i, groups)
        start = pl.multiple_of(peer * nrows + lax.div(i, groups) * LOAD, LOAD)
        slot = lax.rem(i, 2)
        return pltpu.make_async_copy(field.at[:, pl.ds(start, LOAD), :], buf.at[slot], load.at[slot])

    block_load(0).start()

    barrier = pltpu.get_barrier_semaphore()

    def greet(device):
        pl.semaphore_signal(barrier, inc=1, device_id=device, device_id_type=pl.DeviceIdType.MESH)

    for peer in peers:
        greet({"mode": peer})

    @pl.when(jnp.logical_and(me == 0, has_prev))
    def _():
        for j in range(groups):
            greet({"mesh": part - 1, "mode": j})

    @pl.when(jnp.logical_and(me == groups - 1, has_next))
    def _():
        for j in range(groups):
            greet({"mesh": part + 1, "mode": j})

    pl.semaphore_wait(barrier, groups - 1 + has_prev.astype(jnp.int32) + has_next.astype(jnp.int32))

    before = {
        "mesh": jnp.where(me == 0, part - 1, part),
        "mode": lax.rem(me + groups - 1, groups),
    }
    after = {
        "mesh": jnp.where(me == groups - 1, part + 1, part),
        "mode": lax.rem(me + 1, groups),
    }
    kap_after = remote(kap, kext.at[0], send_kap.at[0], recv_kap.at[0], after)
    kap_before = remote(kap, kext.at[1], send_kap.at[1], recv_kap.at[1], before)

    @pl.when(closes)
    def _():
        kap_after.start()

    @pl.when(opens)
    def _():
        kap_before.start()

    def send_block(i, carry):
        block_load(i).wait()

        @pl.when(i + 1 < blocks * groups)
        def _():
            block_load(i + 1).start()

        peer = lax.rem(me + middle + i, groups)
        h = lax.div(i, groups)
        start = peer * nrows + h * LOAD
        slot = lax.rem(i, 2)
        for q in range(0, owned, 16):
            stage[pl.ds(start, LOAD), q : q + 16, :] = jnp.swapaxes(buf[slot, q : q + 16], 0, 1).astype(stage.dtype)
        rows = stage.at[pl.ds(start, LOAD)]
        there = gath.at[pl.ds(1 + h * LOAD, LOAD), mine, :]

        @pl.when(peer != me)
        def _():
            remote(rows, there, send_in, recv_rows.at[h], {"mode": peer}).start()

        @pl.when(peer == me)
        def _():
            pltpu.make_async_copy(rows, there, recv_rows.at[h]).start()

        return carry

    lax.fori_loop(0, blocks * groups, send_block, 0)

    top = gath.at[pl.ds(0, 1)]
    bottom = gath.at[pl.ds(nrows + 1, 1)]
    my_top = gath.at[pl.ds(0, 1), mine, :]
    my_bottom = gath.at[pl.ds(nrows + 1, 1), mine, :]
    centre = middle * nrows
    above = stage.at[pl.ds(centre - 1, 1)]
    below = stage.at[pl.ds(centre, 1)]
    edges = [
        (me != middle, remote(above, my_top, send_edge.at[0], recv_halo.at[0], {"mode": middle})),
        (me != middle - 1, remote(below, my_bottom, send_edge.at[1], recv_halo.at[1], {"mode": middle - 1})),
        (
            has_next,
            remote(
                stage.at[pl.ds(total_rows - 1, 1)], my_top, send_edge.at[2], recv_halo.at[0],
                {"mesh": part + 1, "mode": 0},
            ),
        ),
        (
            has_prev,
            remote(
                stage.at[pl.ds(0, 1)], my_bottom, send_edge.at[3], recv_halo.at[1],
                {"mesh": part - 1, "mode": groups - 1},
            ),
        ),
    ]
    for wanted, copy in edges:
        pl.when(wanted)(copy.start)

    @pl.when(me == middle)
    def _():
        pltpu.make_async_copy(above, my_top, recv_halo.at[0]).start()

    @pl.when(me == middle - 1)
    def _():
        pltpu.make_async_copy(below, my_bottom, recv_halo.at[1]).start()

    @pl.when(jnp.logical_not(opens))
    def _():
        gath[0] = jnp.zeros((modes, width), gath.dtype)
        kext[0] = jnp.zeros(kap.shape, kap.dtype)

    @pl.when(jnp.logical_not(closes))
    def _():
        gath[nrows + 1] = jnp.zeros((modes, width), gath.dtype)
        kext[1] = jnp.zeros(kap.shape, kap.dtype)

    @pl.when(opens)
    def _():
        arrived(kext.at[0], recv_kap.at[0])

    @pl.when(closes)
    def _():
        arrived(kext.at[1], recv_kap.at[1])

    at_row = lax.broadcasted_iota(jnp.int32, (nrows, width), 0)
    at_col = lax.broadcasted_iota(jnp.int32, (nrows, width), 1)
    for k in range(terms):
        c = kap[k].astype(jnp.float32)
        up = kext[0, k].astype(jnp.float32)[nrows - 1 :, :]
        down = kext[1, k].astype(jnp.float32)[:1, :]
        near = (
            jnp.where(at_row == 0, up, pltpu.roll(c, 1, 0)),
            jnp.where(at_row == nrows - 1, down, pltpu.roll(c, nrows - 1, 0)),
            jnp.where(at_col == 0, 0.0, pltpu.roll(c, 1, 1)),
            jnp.where(at_col == width - 1, 0.0, pltpu.roll(c, width - 1, 1)),
        )
        for d in range(4):
            coef[4 * k + d] = 0.5 * (c + near[d])

    cols = lax.broadcasted_iota(jnp.int32, (BAND, width), 1)
    first = cols == 0
    last = cols == width - 1

    def row(r):
        here = pl.ds(r, 1)

        @pl.loop(0, modes // BAND)
        def _(b):
            band = pl.ds(pl.multiple_of(b * BAND, BAND), BAND)
            v = gath[r + 1, band, :].astype(jnp.float32)
            diffs = (
                v - gath[r, band, :].astype(jnp.float32),
                v - gath[r + 2, band, :].astype(jnp.float32),
                v - jnp.where(first, 0.0, pltpu.roll(v, 1, 1)),
                v - jnp.where(last, 0.0, pltpu.roll(v, width - 1, 1)),
            )
            for k in range(terms):
                total = coef[4 * k, here, :] * diffs[0]
                for d in range(1, 4):
                    total = total + coef[4 * k + d, here, :] * diffs[d]
                img[k, band, :] = total.astype(jnp.bfloat16)

        @pl.loop(0, width // TILE)
        def _(t):
            tile = pl.ds(pl.multiple_of(t * TILE, TILE), TILE)
            temps = jnp.dot(tp[...], gath[r + 1, :, tile], preferred_element_type=jnp.float32)
            half = lat[...] * 0.5
            heat = (cap[...] * temps + (half + half * jnp.tanh(temps))).astype(jnp.bfloat16)
            enthalpy = jnp.dot(fp[...], heat, preferred_element_type=jnp.float32)
            mixed = jnp.dot(kl[0], img[0, :, tile], preferred_element_type=jnp.float32)
            for k in range(1, terms):
                mixed = mixed + jnp.dot(kl[k], img[k, :, tile], preferred_element_type=jnp.float32)
            res[r, :, tile] = (mass[here, tile] * enthalpy + mixed).astype(jnp.bfloat16)

    gives_after = jnp.logical_and(me != middle - 1, me != groups - 1)
    gives_before = jnp.logical_and(me != middle, me != 0)
    fwd_after = remote(
        gath.at[pl.ds(nrows, 1)], top, send_fwd.at[0], recv_halo.at[0], {"mode": lax.rem(me + 1, groups)}
    )
    fwd_before = remote(
        gath.at[pl.ds(1, 1)], bottom, send_fwd.at[1], recv_halo.at[1], {"mode": lax.rem(me + groups - 1, groups)}
    )

    arrived(gath.at[pl.ds(1, LOAD)], recv_rows.at[0])
    pl.when(gives_before)(fwd_before.start)

    def step(t, carry):
        @pl.when(jnp.logical_and(lax.rem(t + 2, LOAD) == 0, t < nrows - 2))
        def _():
            h = lax.div(t + 2, LOAD)
            arrived(gath.at[pl.ds(1 + h * LOAD, LOAD)], recv_rows.at[h])

        @pl.when(jnp.logical_and(t == (blocks - 1) * LOAD - 2, gives_after))
        def _():
            fwd_after.start()

        @pl.when(jnp.logical_and(t == nrows - 2, opens))
        def _():
            arrived(top, recv_halo.at[0])

        @pl.when(jnp.logical_and(t == nrows - 1, closes))
        def _():
            arrived(bottom, recv_halo.at[1])

        r = jnp.where(t < nrows - 2, t + 1, (t - (nrows - 2)) * (nrows - 1))
        row(r)
        here = pl.ds(r, 1)
        there = out.at[pl.ds(me * nrows + r, 1)]
        for peer in [peers[(s + middle - 1) % (groups - 1)] for s in range(groups - 1)]:
            part_of = res.at[here, pl.ds(pl.multiple_of(peer * owned, owned), owned), :]
            remote(part_of, there, send_out, recv_out, {"mode": peer}).start()
        pltpu.make_async_copy(res.at[here, mine, :], there, recv_out).start()
        return carry

    lax.fori_loop(0, nrows, step, 0)

    pl.when(closes)(kap_after.wait_send)
    pl.when(opens)(kap_before.wait_send)
    for wanted, copy in edges:
        pl.when(wanted)(copy.wait_send)
    pl.when(gives_after)(fwd_after.wait_send)
    pl.when(gives_before)(fwd_before.wait_send)
    arrived(gath.at[pl.ds(0, nrows), others, :], send_in)
    arrived(res.at[:, others, :], send_out)
    arrived(out, recv_out)


def exchange(field, kappa, mass, kl, tp, fp, cap, lat):
    groups, parts = lax.axis_size("mode"), lax.axis_size("mesh")
    owned, total_rows, width = field.shape
    nrows, modes = mass.shape[0], tp.shape[1]
    terms = kl.shape[0]
    vmem = pl.BlockSpec(memory_space=pltpu.VMEM)
    hbm = pl.BlockSpec(memory_space=pl.ANY)
    work = modes * nrows * width
    dma = pltpu.SemaphoreType.DMA
    return pl.pallas_call(
        functools.partial(kernel, groups, parts),
        out_shape=jax.ShapeDtypeStruct((total_rows, owned, width), jnp.bfloat16),
        in_specs=[hbm] + [vmem] * 7,
        out_specs=hbm,
        scratch_shapes=[
            pltpu.VMEM((2, owned, LOAD, width), jnp.float32),
            pltpu.VMEM((total_rows, owned, width), jnp.bfloat16),
            pltpu.VMEM((nrows + 2, modes, width), jnp.bfloat16),
            pltpu.VMEM((nrows, modes, width), jnp.bfloat16),
            pltpu.VMEM((terms, modes, width), jnp.bfloat16),
            pltpu.VMEM((terms * 4, nrows, width), jnp.float32),
            pltpu.VMEM((2,) + kappa.shape, jnp.bfloat16),
            dma((2,)),
            dma((nrows // LOAD,)),
            dma((2,)),
            dma((2,)),
            dma,
            dma,
            dma((4,)),
            dma((2,)),
            dma((2,)),
            dma,
        ],
        compiler_params=pltpu.CompilerParams(
            collective_id=0, has_side_effects=True, vmem_limit_bytes=48 * 1024 * 1024
        ),
        cost_estimate=pl.CostEstimate(
            flops=2 * work * (terms * modes + 2 * tp.shape[0]),
            bytes_accessed=6 * work,
            transcendentals=nrows * width * tp.shape[0],
        ),
    )(field, kappa, mass, kl, tp, fp, cap[:, None], lat[:, None])


def exchange_small(ext, coef, mass, kl, tp, fp, cap, lat):
    groups = lax.axis_size("mode")
    owned, width = ext.shape[1:]
    nrows, modes = mass.shape[0], tp.shape[1]
    terms = coef.shape[1] // 4
    parts = jnp.stack([ext[d * nrows : d * nrows + nrows + 2] for d in range(groups)], 0)
    moved = lax.all_to_all(parts, "mode", split_axis=0, concat_axis=0, tiled=True)
    rows = jnp.moveaxis(moved, 0, 1).reshape(nrows + 2, modes, width)
    own = rows[1:-1]
    v = jnp.pad(rows.astype(jnp.float32), ((0, 0), (0, 0), (1, 1)))
    centre = v[1:-1, :, 1:-1]
    others = (v[:-2, :, 1:-1], v[2:, :, 1:-1], v[1:-1, :, :-2], v[1:-1, :, 2:])
    images = [
        sum(coef[:, 4 * k + d, None, :] * (centre - others[d]) for d in range(4)).astype(jnp.bfloat16)
        for k in range(terms)
    ]
    images = jnp.concatenate(images, 1)
    mixed = jnp.einsum("ij,rjx->rix", kl, images, preferred_element_type=jnp.float32)
    temps = jnp.einsum("qi,rix->rqx", tp, own, preferred_element_type=jnp.float32)
    heat = (cap[:, None] * temps + lat[:, None] * jax.nn.sigmoid(2.0 * temps)).astype(jnp.bfloat16)
    enthalpy = jnp.einsum("iq,rqx->rix", fp, heat, preferred_element_type=jnp.float32)
    result = (mass[:, None, :] * enthalpy + mixed).astype(jnp.bfloat16)
    result = result.reshape(nrows, groups, owned, width)
    back = lax.all_to_all(result, "mode", split_axis=1, concat_axis=0, tiled=True)
    return back.reshape(nrows * groups, owned, width)


def body(field, kappa, mass, kl_modes, to_points, from_points, capacity, latent):
    nrows, owned = mass.shape[0], field.shape[0]
    fits = owned % 16 == 0 and nrows % 16 == 0 and field.shape[2] % TILE == 0
    if fits:
        out = exchange(field, kappa, mass, kl_modes, to_points, from_points, capacity, latent)
        return jnp.transpose(out, (1, 0, 2))
    coarse = jnp.transpose(field.astype(jnp.bfloat16), (1, 0, 2))
    up, down = halo(coarse, "mesh")
    ext = jnp.concatenate([up, coarse, down], 0)
    coef = weights_of(kappa)
    terms, modes = kl_modes.shape[:2]
    kl = jnp.transpose(kl_modes, (1, 0, 2)).reshape(modes, terms * modes)
    out = exchange_small(ext, coef, mass, kl, to_points, from_points, capacity, latent)
    return jnp.transpose(out, (1, 0, 2))


def solution(mesh):
    in_specs = (
        P("mode", "mesh", None),
        P(None, ("mesh", "mode"), None),
        P(("mesh", "mode"), None),
        P(),
        P(),
        P(),
        P(),
        P(),
    )
    out_specs = P("mode", "mesh", None)
    return jax.shard_map(body, mesh=mesh, in_specs=in_specs, out_specs=out_specs, check_vma=False)
```

time: 443 us -> 396 us (0.89); the launches traced: 436 us -> 395 us
  local copies, waits for them, and re-layouts: 33.3 us -> 17.8 us
  starting transfers between devices: 13.3 us -> 0 us
  other arithmetic: 7.73 us -> 0 us
    unnamed x18 -> x10, local copies, waits for them, and re-layouts: 20 us -> 4.62 us
    ppermute x4 -> x0, starting transfers between devices: 13.3 us -> none  [the longest x2 10.5 us: halo(): up = lax.ppermute(rows[-1:], axes, [(i, i + 1) for i in range(count - 1)])]
    concatenate x1 -> x0, other arithmetic: 7.43 us -> none  [body(): ext = jnp.concatenate([up, coarse, down], 0)]
  transfers between devices with their start and end apart: 4 -> 0, of which waited for: 1 -> 0; matrix products, arithmetic and copies ran while one was open for 4% -> 0% of each run, Pallas kernels for 0% -> 0%
where the time goes in v2:
time: 396 us; the launch traced here: 395 us
  Pallas kernels  378 us (95%)
  local copies, waits for them, and re-layouts  17.8 us (4%)
    pallas_call x1, Pallas kernels, exchange(): pl.pallas_call(functools.partial(kernel, groups, parts), out_shape=jax.Sh...  378 us
    transpose x1, local copies, waits for them, and re-layouts, body(): return jnp.transpose(out, (1, 0, 2))  11.5 us

profile of v2, /device:TPU:0, one launch (start us, length us, event | category | flops | bytes accessed | tf_op | source)
XLA Modules:
  0.0 395.3 jit_solution(16228812364306137895)
XLA Ops:
  0.0 0.8 copy.10.cap
  0.8 0.8 copy.11.lat
  1.7 0.0 copy-start
  1.7 1.0 copy-done
  2.7 0.0 copy-start.1
  2.7 0.9 copy-done.1
  3.6 0.0 copy-start.2
  3.6 0.9 copy-done.2
  4.6 0.0 copy-start.3
  4.6 0.9 copy-done.3
  5.5 0.0 copy-start.4
  5.5 0.8 copy-done.4
  6.3 377.5 %shard_map.82 = bf16[128,32,1024]{2,1,0:T(8,128)(2,1)} custom-call(f32[32,128,1024]{2,1,0:T(8,128)} %field.1, bf16[3,16,1024]{2,1,0:T(8,128)(2,1)S(1)} %copy-done.3, f32[16,1024]{1,0:T(8,128)S(1)} %copy-done.4, bf16[3,256,256]{2,1,0:T(8,128)(2,1)S(1)} %copy-done, bf16[512,256]{1,0:T(8,128)(2,1)S(1)} %copy-done.1, bf16[256,512]{1,0:T(8,128)(2,1)S(1)} %copy-done.2, ...), custom_call_target="tpu_custom_call" | custom-call | flops 15032385536 | bytes 25165824 | tf_op jit(solution)/shard_map/pallas_call | solution.py:305
  383.8 11.5 %copy.12 = bf16[32,128,1024]{2,1,0:T(8,128)(2,1)} copy(bf16[32,128,1024]{2,0,1:T(8,128)(2,1)} %bitcast.3) | data formatting | bytes 16777216 | tf_op jit(solution)/shard_map/transpose | solution.py:372
Async XLA Ops:
  1.7 1.0 copy-start
  2.7 0.9 copy-start.1
  3.6 0.9 copy-start.2
  4.6 0.9 copy-start.3
  5.5 0.8 copy-start.4

commit v3 on v2

--- a/solution.py
+++ b/solution.py
@@ -31,9 +31,9 @@
 
 
 def kernel(
-    groups, parts, field, kap, mass, kl, tp, fp, cap, lat, out,
-    buf, stage, gath, res, img, coef, kext,
-    load, recv_rows, recv_halo, recv_kap, recv_out, send_in, send_edge, send_fwd, send_kap, send_out,
+    groups, parts, field, kap, mass, kl_all, tp_all, fp_all, cap, lat, out,
+    buf, stage, gath, res, img, coef, kext, kl, tp, fp,
+    load, recv_rows, recv_halo, recv_kap, recv_out, send_in, send_edge, send_fwd, send_kap, send_out, fetch,
 ):
     me = lax.axis_index("mode")
     part = lax.axis_index("mesh")
@@ -61,13 +61,24 @@
     def arrived(ref, sem):
         pltpu.make_async_copy(ref, ref, sem).wait()
 
+    way = 1 - 2 * lax.rem(part, 2)
+
+    def partner(i):
+        return lax.rem(me + middle + groups + way * lax.rem(i, groups), groups)
+
     def block_load(i):
-        peer = lax.rem(me + middle + i, groups)
+        peer = partner(i)
         start = pl.multiple_of(peer * nrows + lax.div(i, groups) * LOAD, LOAD)
         slot = lax.rem(i, 2)
         return pltpu.make_async_copy(field.at[:, pl.ds(start, LOAD), :], buf.at[slot], load.at[slot])
 
     block_load(0).start()
+    fetches = [
+        pltpu.make_async_copy(whole, held, fetch.at[n])
+        for n, (whole, held) in enumerate(((kl_all, kl), (tp_all, tp), (fp_all, fp)))
+    ]
+    for copy in fetches:
+        copy.start()
 
     barrier = pltpu.get_barrier_semaphore()
 
@@ -115,7 +126,7 @@
         def _():
             block_load(i + 1).start()
 
-        peer = lax.rem(me + middle + i, groups)
+        peer = partner(i)
         h = lax.div(i, groups)
         start = peer * nrows + h * LOAD
         slot = lax.rem(i, 2)
@@ -249,6 +260,8 @@
         gath.at[pl.ds(1, 1)], bottom, send_fwd.at[1], recv_halo.at[1], {"mode": lax.rem(me + groups - 1, groups)}
     )
 
+    for copy in fetches:
+        copy.wait()
     arrived(gath.at[pl.ds(1, LOAD)], recv_rows.at[0])
     pl.when(gives_before)(fwd_before.start)
 
@@ -274,7 +287,7 @@
         row(r)
         here = pl.ds(r, 1)
         there = out.at[pl.ds(me * nrows + r, 1)]
-        for peer in [peers[(s + middle - 1) % (groups - 1)] for s in range(groups - 1)]:
+        for peer in [partner(s) for s in range(groups) if s != middle]:
             part_of = res.at[here, pl.ds(pl.multiple_of(peer * owned, owned), owned), :]
             remote(part_of, there, send_out, recv_out, {"mode": peer}).start()
         pltpu.make_async_copy(res.at[here, mine, :], there, recv_out).start()
@@ -305,7 +318,7 @@
     return pl.pallas_call(
         functools.partial(kernel, groups, parts),
         out_shape=jax.ShapeDtypeStruct((total_rows, owned, width), jnp.bfloat16),
-        in_specs=[hbm] + [vmem] * 7,
+        in_specs=[hbm, vmem, vmem, hbm, hbm, hbm, vmem, vmem],
         out_specs=hbm,
         scratch_shapes=[
             pltpu.VMEM((2, owned, LOAD, width), jnp.float32),
@@ -315,6 +328,9 @@
             pltpu.VMEM((terms, modes, width), jnp.bfloat16),
             pltpu.VMEM((terms * 4, nrows, width), jnp.float32),
             pltpu.VMEM((2,) + kappa.shape, jnp.bfloat16),
+            pltpu.VMEM(kl.shape, kl.dtype),
+            pltpu.VMEM(tp.shape, tp.dtype),
+            pltpu.VMEM(fp.shape, fp.dtype),
             dma((2,)),
             dma((nrows // LOAD,)),
             dma((2,)),
@@ -325,6 +341,7 @@
             dma((2,)),
             dma((2,)),
             dma,
+            dma((3,)),
         ],
         compiler_params=pltpu.CompilerParams(
             collective_id=0, has_side_effects=True, vmem_limit_bytes=48 * 1024 * 1024

time: 396 us -> 394 us (level)
  no operation moved by 1% of the time
where the time goes in v3:
time: 394 us; the launch traced here: 393 us
  Pallas kernels  376 us (95%)
  local copies, waits for them, and re-layouts  17.8 us (5%)
    pallas_call x1, Pallas kernels, exchange(): pl.pallas_call(functools.partial(kernel, groups, parts), out_shape=jax.Sh...  376 us
    transpose x1, local copies, waits for them, and re-layouts, body(): return jnp.transpose(out, (1, 0, 2))  11.5 us

profile of v3, /device:TPU:0, one launch (start us, length us, event | category | flops | bytes accessed | tf_op | source)
XLA Modules:
  0.0 393.5 jit_solution(2444777183326304615)
XLA Ops:
  0.0 0.8 copy.10.cap
  0.8 0.8 copy.11.lat
  1.7 0.0 copy-start
  1.7 1.0 copy-done
  2.7 0.0 copy-start.1
  2.7 0.9 copy-done.1
  3.6 0.0 copy-start.2
  3.6 0.9 copy-done.2
  4.6 0.0 copy-start.3
  4.6 0.9 copy-done.3
  5.5 0.0 copy-start.4
  5.5 0.8 copy-done.4
  6.3 375.7 %shard_map.82 = bf16[128,32,1024]{2,1,0:T(8,128)(2,1)} custom-call(f32[32,128,1024]{2,1,0:T(8,128)} %field.1, bf16[3,16,1024]{2,1,0:T(8,128)(2,1)S(1)} %copy-done.3, f32[16,1024]{1,0:T(8,128)S(1)} %copy-done.4, bf16[3,256,256]{2,1,0:T(8,128)(2,1)S(1)} %copy-done, bf16[512,256]{1,0:T(8,128)(2,1)S(1)} %copy-done.1, bf16[256,512]{1,0:T(8,128)(2,1)S(1)} %copy-done.2, ...), custom_call_target="tpu_custom_call" | custom-call | flops 15032385536 | bytes 25165824 | tf_op jit(solution)/shard_map/pallas_call | solution.py:318
  382.0 11.5 %copy.12 = bf16[32,128,1024]{2,1,0:T(8,128)(2,1)} copy(bf16[32,128,1024]{2,0,1:T(8,128)(2,1)} %bitcast.3) | data formatting | bytes 16777216 | tf_op jit(solution)/shard_map/transpose | solution.py:389
Async XLA Ops:
  1.7 1.0 copy-start
  2.7 0.9 copy-start.1
  3.6 0.9 copy-start.2
  4.6 0.9 copy-start.3
  5.5 0.8 copy-start.4
